TPU v7x, 256 devices: a whole 4x4x8 slice. The times are simulated.
256 devices in a mesh: row: 32 (over z_lo, x, y), col: 8 (over z_hi, core).
Axes of the slice: x: 4, y: 4, z: 8 (z_hi: 4, z_lo: 2; z = z_hi * 2 + z_lo), core: 2. Of those that a mesh axis runs over, the one named last changes fastest.
Arguments:
- grad_out: bfloat16 [64, 512, 2048], P(None, 'row', 'col'), may hold values from -6 to 6
- row_feat: bfloat16 [512, 64], P('row'), may hold values from -6 to 6
- col_feat: bfloat16 [2048, 64], P('col'), may hold values from -6 to 6
- conv_one: bfloat16 [3, 3, 64, 64], replicated, may hold values from -0.25 to 0.25
- bias_one: float32 [64], replicated, may hold values from -3 to 3
- conv_two: bfloat16 [3, 3, 64, 64], replicated, may hold values from -0.25 to 0.25
Outputs:
- row_grad: float32 [512, 64], P('row')
- col_grad: float32 [2048, 64], P('col')
- grad_conv_one: float32 [3, 3, 64, 64], replicated
- grad_bias: float32 [64], replicated
- grad_conv_two: float32 [3, 3, 64, 64], replicated
All inputs are finite; a program needn't handle non-finite values.
Results may differ from a plain program's by a relative error of at most 0.0065.
Values may be sent and summed in bfloat16 or wider, within the bound.
No kernel may reach another device: no remote copies, remote signals or barrier semaphores. Data moves between devices by JAX's collectives and lax.ppermute only.
A program may use at most 128 MiB of HBM per device.

v0:
```python
import math
import jax
import jax.numpy as jnp
from jax import lax
from jax.sharding import PartitionSpec as P


def extended(block, sides, width):
    for axis, dim in sides:
        count = lax.axis_size(axis)
        forward = [(i, i + 1) for i in range(count - 1)]
        backward = [(target, source) for source, target in forward]
        low = lax.ppermute(
            lax.slice_in_dim(block, block.shape[dim] - width, None, axis=dim), axis, forward
        )
        high = lax.ppermute(lax.slice_in_dim(block, 0, width, axis=dim), axis, backward)
        block = jnp.concatenate([low, block, high], axis=dim)
    return block


def conv_valid(kernel, field):
    result = lax.conv_general_dilated(
        field[None],
        kernel,
        (1, 1),
        "VALID",
        rhs_dilation=(8, 8),
        dimension_numbers=("NCHW", "HWOI", "NCHW"),
        preferred_element_type=jnp.float32,
    )
    return result[0]


def flipped(kernel):
    return jnp.transpose(kernel[::-1, ::-1], (0, 1, 3, 2))


def tap_grads(upper, field, base_r, base_c, rows, cols):
    taps = []
    for tap_r in range(3):
        line = []
        for tap_c in range(3):
            top = base_r + 8 * (tap_r - 1)
            left = base_c + 8 * (tap_c - 1)
            piece = field[:, top : top + rows, left : left + cols]
            line.append(
                lax.dot_general(
                    upper, piece, (((1, 2), (1, 2)), ((), ())), preferred_element_type=jnp.float32
                )
            )
        taps.append(jnp.stack(line))
    return jnp.stack(taps)


def slope(pre):
    sig = jax.nn.sigmoid(pre)
    return sig * (1.0 + pre * (1.0 - sig))


def inside_mask(row_first, col_first, margin, tile_rows, tile_cols, total_rows, total_cols):
    global_rows = row_first + jnp.arange(tile_rows + 2 * margin, dtype=jnp.int32) - margin
    global_cols = col_first + jnp.arange(tile_cols + 2 * margin, dtype=jnp.int32) - margin
    return ((global_rows >= 0) & (global_rows < total_rows))[:, None] & (
        (global_cols >= 0) & (global_cols < total_cols)
    )[None, :]


def shards(grad_out, row_feat, col_feat, conv_one, bias_one, conv_two):
    chans, tile_rows, tile_cols = grad_out.shape
    total_rows = tile_rows * lax.axis_size("row")
    total_cols = tile_cols * lax.axis_size("col")
    row_first = lax.axis_index("row") * tile_rows
    col_first = lax.axis_index("col") * tile_cols
    row_ext = extended(row_feat, (("row", 0),), 16)
    col_ext = extended(col_feat, (("col", 0),), 16)
    outer = inside_mask(row_first, col_first, 16, tile_rows, tile_cols, total_rows, total_cols)
    summed = row_ext.T.astype(jnp.float32)[:, :, None] + col_ext.T.astype(jnp.float32)[:, None, :]
    field = jnp.where(outer[None], summed, 0.0).astype(jnp.bfloat16)
    pre = conv_valid(conv_one, field) + bias_one[:, None, None]
    inside = inside_mask(row_first, col_first, 8, tile_rows, tile_cols, total_rows, total_cols)
    act = jnp.where(inside[None], jax.nn.silu(pre), 0.0).astype(jnp.bfloat16)
    grad_ext = extended(grad_out, (("row", 1), ("col", 2)), 16)
    back = conv_valid(flipped(conv_two), grad_ext)
    inner = jnp.where(inside[None], back * slope(pre), 0.0).astype(jnp.bfloat16)
    spread = conv_valid(flipped(conv_one), inner)
    inner_tile = inner[:, 8 : 8 + tile_rows, 8 : 8 + tile_cols]
    grad_in = grad_out.astype(jnp.float32) + spread
    row_part = jnp.sum(grad_in, axis=2).T
    col_part = jnp.sum(grad_in, axis=1).T
    grad_one = tap_grads(inner_tile, field, 16, 16, tile_rows, tile_cols)
    grad_two = tap_grads(grad_out, act, 8, 8, tile_rows, tile_cols)
    bias_part = jnp.sum(inner_tile.astype(jnp.float32), axis=(1, 2))
    row_grad = lax.psum(row_part, "col") / math.sqrt(total_cols)
    col_grad = lax.psum(col_part, "row") / math.sqrt(total_rows)
    sum_one, sum_bias, sum_two = lax.psum((grad_one, bias_part, grad_two), ("row", "col"))
    whole = math.sqrt(total_rows * total_cols)
    return (row_grad, col_grad, sum_one / whole, sum_bias / whole, sum_two / whole)


def solution(mesh):
    in_specs = (P(None, "row", "col"), P("row", None), P("col", None), P(), P(), P())
    out_specs = (P("row", None), P("col", None), P(), P(), P())
    return jax.shard_map(shards, mesh=mesh, in_specs=in_specs, out_specs=out_specs, check_vma=False)
```

profile of v0, /device:TPU:1, one launch (start us, length us, event | category | flops | bytes accessed | tf_op | source)
XLA Modules:
  0.0 769.2 jit_solution(11806747635135335982)
XLA Ops:
  7.2 4.2 collective-permute-start.4
  11.4 1.3 collective-permute-start.5
  12.7 0.8 fusion.84
  13.5 5.7 collective-permute-start.6
  19.3 1.9 collective-permute-start.7
  21.2 5.1 collective-permute-start
  26.5 3.6 copy.67
  30.4 1.3 collective-permute-start.1
  31.7 0.8 convert_bitcast_fusion
  32.7 0.7 convert_bitcast_fusion.1
  33.4 2.7 select_convert_fusion
  36.1 2.3 copy.77
  39.3 5.9 broadcast_select_fusion
  45.2 2.7 copy.84
  47.9 2.6 slice.105
  50.5 6.2 copy.124
  56.7 3.2 select_convert_fusion.2
  63.5 2.3 select_convert_fusion.1
  66.5 3.8 add_divide_fusion
  70.3 3.5 copy.69
  73.8 3.6 copy.71
  77.4 1.2 pad_maximum_fusion.5
  78.7 4.8 collective-permute-start.2
  83.5 1.9 collective-permute-start.3
  85.4 0.7 pad_maximum_fusion.2
  86.2 5.2 collective-permute-done.3
  91.4 5.1 pad_maximum_fusion
  96.5 2.3 copy.73
  99.4 6.2 multiply_multiply_fusion
  105.5 2.7 copy.82
  108.3 2.5 slice.104
  110.8 6.1 copy.123
  116.9 3.8 convert_reduce_fusion
  124.1 86.2 %psum.38 = f32[64]{0:T(128)S(1)} all-reduce(f32[64]{0:T(128)S(1)} %get-tuple-element.14), channel_id=1, replica_groups=mesh['row'=32,'col'=8] {'row','col'}, use_global_device_ids=true, to_apply=%region_6.7 | all-reduce | flops 64 | bytes 512 | tf_op jit(solution)/shard_map/psum | solution.py:95
  210.7 0.9 copy.78
  211.6 2.2 fusion.17
  213.9 1.4 copy.80
  215.7 2.0 fusion.33
  217.7 0.7 copy.81
  219.0 1.4 fusion.36
  220.4 14.5 %psum.35 = f32[16,64]{1,0:T(8,128)S(1)} all-reduce(f32[16,64]{1,0:T(8,128)S(1)} %bitcast.166), channel_id=1, replica_groups=mesh['row'=32,'col'=8] {'col'}, use_global_device_ids=true, to_apply=%region_1.2 | all-reduce | flops 1024 | bytes 8192 | tf_op jit(solution)/shard_map/psum | solution.py:93
  235.5 0.7 pad_maximum_fusion.1
  236.3 250.7 %all-reduce.4.cloned.1.call-done = f32[256,64]{1,0:T(8,128)} async-done(((f32[256,64]{1,0:T(8,128)}), f32[256,64]{1,0:T(8,128)}) %all-reduce.4.cloned.1.call-update) | async-done | bytes 65552 | tf_op jit(solution)/shard_map/psum | solution.py:94
  487.0 0.9 broadcast_multiply_fusion.2
  487.9 0.7 copy.104
  488.6 270.1 %all-reduce.6.cloned.1.call-done = (f32[3,3,64,64]{3,2,1,0:T(8,128)}, f32[3,3,64,64]{3,2,1,0:T(8,128)}) async-done(((f32[3,3,64,64]{3,2,1,0:T(8,128)}, f32[3,3,64,64]{3,2,1,0:T(8,128)}), (f32[3,3,64,64]{3,2,1,0:T(8,128)}, f32[3,3,64,64]{3,2,1,0:T(8,128)})) %all-reduce.6.cloned.1.call-update) | async-done | bytes 294928 | tf_op jit(solution)/shard_map/psum | solution.py:95
  758.7 1.7 broadcast_multiply_fusion
  760.4 1.7 broadcast_multiply_fusion.1
  (85 shorter events, 11.6 us)
Async XLA Ops:
  7.2 92.2 %copy-start = (bf16[3,3,64,64]{3,2,1,0:T(8,128)(2,1)S(1)}, bf16[3,3,64,64]{3,2,1,0:T(8,128)(2,1)}, u32[]{:S(2)}) copy-start(bf16[3,3,64,64]{3,2,1,0:T(8,128)(2,1)} %param.11) | copy-start | bytes 221188
  7.2 479.8 %all-reduce.4.cloned.1.call-start = ((), (), s32[]{:S(2)}) async-start(), calls=%async_computation | async-start | bytes 262144 | tf_op jit(solution)/shard_map/psum | solution.py:94
  7.2 25.5 %collective-permute-start.4 = (bf16[16,64]{1,0:T(8,128)(2,1)}, bf16[16,64]{1,0:T(8,128)(2,1)S(1)}, u32[]{:S(2)}, u32[]{:S(2)}) collective-permute-start(bf16[16,64]{1,0:T(8,128)(2,1)} %param.7), channel_id=1, source_target_pairs={{0,8},{8,16},{16,24},{24,32},{32,40},{40,48},{48,56},{56,64},{64,7... | collective-permute-start | bytes 6152 | tf_op jit(solution)/shard_map/ppermute | solution.py:13
  11.4 21.3 %collective-permute-start.5 = (bf16[16,64]{1,0:T(8,128)(2,1)}, bf16[16,64]{1,0:T(8,128)(2,1)S(1)}, u32[]{:S(2)}, u32[]{:S(2)}) collective-permute-start(bf16[16,64]{1,0:T(8,128)(2,1)} %param.7), channel_id=1, source_target_pairs={{8,0},{16,8},{24,16},{32,24},{40,32},{48,40},{56,48},{64,56},{72,6... | collective-permute-start | bytes 6152 | tf_op jit(solution)/shard_map/ppermute | solution.py:16
  13.5 16.9 %collective-permute-start.6 = (bf16[16,64]{0,1:T(8,128)(2,1)S(1)}, bf16[16,64]{0,1:T(8,128)(2,1)S(1)}, u32[]{:S(2)}, u32[]{:S(2)}) collective-permute-start(bf16[16,64]{0,1:T(8,128)(2,1)S(1)} %get-tuple-element.22), channel_id=1, source_target_pairs={{0,1},{1,2},{2,3},{3,4},{4,5},{5,6},{6,7},{8,9},{9,10},{10,11},{11... | collective-permute-start | bytes 6152 | tf_op jit(solution)/shard_map/ppermute | solution.py:13
  19.3 12.5 %collective-permute-start.7 = (bf16[16,64]{0,1:T(8,128)(2,1)S(1)}, bf16[16,64]{0,1:T(8,128)(2,1)S(1)}, u32[]{:S(2)}, u32[]{:S(2)}) collective-permute-start(bf16[16,64]{0,1:T(8,128)(2,1)S(1)} %get-tuple-element.23), channel_id=1, source_target_pairs={{1,0},{2,1},{3,2},{4,3},{5,4},{6,5},{7,6},{9,8},{10,9},{11,10},{12... | collective-permute-start | bytes 6152 | tf_op jit(solution)/shard_map/ppermute | solution.py:16
  21.2 49.1 %collective-permute-start = (bf16[64,16,256]{2,1,0:T(8,128)(2,1)}, bf16[64,16,256]{2,1,0:T(8,128)(2,1)}, u32[]{:S(2)}, u32[]{:S(2)}) collective-permute-start(bf16[64,16,256]{2,1,0:T(8,128)(2,1)} %param.6), channel_id=1, source_target_pairs={{0,8},{8,16},{16,24},{24,32},{32,40},{40,48},{48,56},{56,64},{64,7... | collective-permute-start | bytes 1572872 | tf_op jit(solution)/shard_map/ppermute | solution.py:13
  30.4 43.4 %collective-permute-start.1 = (bf16[64,16,256]{2,1,0:T(8,128)(2,1)}, bf16[64,16,256]{2,1,0:T(8,128)(2,1)}, u32[]{:S(2)}, u32[]{:S(2)}) collective-permute-start(bf16[64,16,256]{2,1,0:T(8,128)(2,1)} %param.6), channel_id=1, source_target_pairs={{8,0},{16,8},{24,16},{32,24},{40,32},{48,40},{56,48},{64,56},{72,6... | collective-permute-start | bytes 1572872 | tf_op jit(solution)/shard_map/ppermute | solution.py:16
  38.4 0.9 copy-start.12
  38.4 0.9 copy-start.15
  45.2 2.8 copy-start.6
  50.5 6.2 copy-start.11
  56.7 3.2 copy-start.9
  77.4 8.0 %copy-start.10 = (f32[1,3,64,64]{3,2,1,0:T(8,128)S(1)}, f32[1,3,64,64]{3,2,1,0:T(8,128)}, u32[]{:S(2)}) copy-start(f32[1,3,64,64]{3,2,1,0:T(8,128)} %get-tuple-element.29) | copy-start | bytes 147460
  77.4 14.0 %copy-start.2 = (bf16[64,16,256]{0,1,2:T(8,128)(2,1)S(1)}, bf16[64,16,256]{0,1,2:T(8,128)(2,1)}, u32[]{:S(2)}) copy-start(bf16[64,16,256]{0,1,2:T(8,128)(2,1)} %copy.67) | copy-start | bytes 1572868
  77.4 14.0 %copy-start.4 = (bf16[64,16,256]{0,1,2:T(8,128)(2,1)S(1)}, bf16[64,16,256]{0,1,2:T(8,128)(2,1)}, u32[]{:S(2)}) copy-start(bf16[64,16,256]{0,1,2:T(8,128)(2,1)} %copy.69) | copy-start | bytes 1572868
  77.4 14.0 %copy-start.5 = (bf16[64,16,256]{0,1,2:T(8,128)(2,1)S(1)}, bf16[64,16,256]{0,1,2:T(8,128)(2,1)}, u32[]{:S(2)}) copy-start(bf16[64,16,256]{0,1,2:T(8,128)(2,1)} %copy.71) | copy-start | bytes 1572868
  78.7 7.5 collective-permute-start.2
  83.5 7.9 %collective-permute-start.3 = (bf16[64,48,16]{0,1,2:T(8,128)(2,1)S(1)}, bf16[64,48,16]{0,1,2:T(8,128)(2,1)S(1)}, u32[]{:S(2)}, u32[]{:S(2)}) collective-permute-start(bf16[64,48,16]{0,1,2:T(8,128)(2,1)S(1)} %get-tuple-element.21), channel_id=1, source_target_pairs={{1,0},{2,1},{3,2},{4,3},{5,4},{6,5},{7,6},{9,8},{10,9},{11,10},{12... | collective-permute-start | bytes 294920 | tf_op jit(solution)/shard_map/ppermute | solution.py:16
  91.4 7.9 %slice-start = ((s8[4718592]{0:T(1024)(128)(4,1)}), s8[4194304]{0:T(1024)(128)(4,1)S(1)}, s32[]{:S(2)}) async-start(s8[4718592]{0:T(1024)(128)(4,1)} %bitcast.163), calls=%async_computation.2 | async-start | bytes 8388608
  96.5 2.8 slice-start.1
  116.9 3.8 copy-start.7
  121.8 88.9 %copy-start.8 = (bf16[32,8,36,64]{3,1,2,0:T(8,128)(2,1)S(1)}, bf16[32,8,36,64]{3,1,2,0:T(8,128)(2,1)}, u32[]{:S(2)}) copy-start(bf16[32,8,36,64]{3,1,2,0:T(8,128)(2,1)} %get-tuple-element.24) | copy-start | bytes 3538948
  213.9 1.8 copy-start.13
  213.9 1.8 copy-start.14
  217.7 1.2 copy-start.3
  218.5 543.7 %copy-start.1 = (bf16[3,3,64,64]{3,2,1,0:T(8,128)(2,1)S(1)}, bf16[3,3,64,64]{3,2,1,0:T(8,128)(2,1)}, u32[]{:S(2)}) copy-start(bf16[3,3,64,64]{3,2,1,0:T(8,128)(2,1)} %param.11) | copy-start | bytes 221188
  220.4 538.3 %all-reduce.6.cloned.1.call-start = ((), (), s32[]{:S(2)}) async-start(), calls=%async_computation.1 | async-start | bytes 1179648 | tf_op jit(solution)/shard_map/psum | solution.py:95
Sparse Core Ops, SparseCore 0:
  220.5 266.4 all-reduce.3
  494.1 264.5 all-reduce.5
where the time goes:
time: 772 us; the launch traced here: 769 us
  waiting for transfers between devices  526 us (68%)
  blocking collectives  101 us (13%)
  local copies, waits for them, and re-layouts  45.4 us (6%)
  other arithmetic  35.1 us (5%)
  starting transfers between devices  26.3 us (3%)
  matrix products  20.9 us (3%)
  between operations  14.8 us (2%)
    psum x1, waiting for transfers between devices, shards(): lax.psum((grad_one, bias_part, grad_two), ('row', 'col'))  270 us
    psum x1, waiting for transfers between devices, shards(): col_grad = lax.psum(col_part, 'row') / math.sqrt(total_rows)  251 us
    psum x1, blocking collectives, shards(): lax.psum((grad_one, bias_part, grad_two), ('row', 'col'))  86.2 us
    ppermute x4, starting transfers between devices, extended(): lax.ppermute(lax.slice_in_dim(block, block.shape[dim] - width, None, axis...  19.8 us
    conv_general_dilated x11, local copies, waits for them, and re-layouts, conv_valid(): lax.conv_general_dilated(field[None], kernel, (1, 1), 'VALID', rhs_dilati...  18.6 us
    unnamed x40, local copies, waits for them, and re-layouts  17.6 us
  transfers between devices with their start and end apart: 10, of which 3 were waited for; matrix products, arithmetic and copies ran while one was open for 7% of the time, Pallas kernels for 0%

commit v1 on v0

--- a/solution.py
+++ b/solution.py
@@ -92,7 +92,7 @@
     bias_part = jnp.sum(inner_tile.astype(jnp.float32), axis=(1, 2))
     row_grad = lax.psum(row_part, "col") / math.sqrt(total_cols)
     col_grad = lax.psum(col_part, "row") / math.sqrt(total_rows)
-    sum_one, sum_bias, sum_two = lax.psum((grad_one, bias_part, grad_two), ("row", "col"))
+    sum_one, sum_bias, sum_two = lax.psum(lax.psum((grad_one, bias_part, grad_two), "row"), "col")
     whole = math.sqrt(total_rows * total_cols)
     return (row_grad, col_grad, sum_one / whole, sum_bias / whole, sum_two / whole)
 

time: 772 us -> 542 us (0.70)
  waiting for transfers between devices: 526 us -> 298 us
    psum x1, waiting for transfers between devices: 270 us -> 96.6 us  [shards(): lax.psum(lax.psum((grad_one, bias_part, grad_two), 'row'), 'col')]
    psum x1, waiting for transfers between devices: 251 us -> 196 us  [shards(): col_grad = lax.psum(col_part, 'row') / math.sqrt(total_rows)]
    psum x1, blocking collectives: 86.2 us -> 71.9 us  [shards(): lax.psum((grad_one, bias_part, grad_two), 'row')]
    psum x1, blocking collectives: 14.5 us -> 26.7 us  [shards(): row_grad = lax.psum(row_part, 'col') / math.sqrt(total_cols)]
  transfers between devices with their start and end apart: 10 -> 10, of which waited for: 3 -> 3; matrix products, arithmetic and copies ran while one was open for 7% -> 9% of each run, Pallas kernels for 0% -> 0%
where the time goes in v1:
time: 542 us; the launch traced here: 539 us
  waiting for transfers between devices  298 us (55%)
  blocking collectives  98.6 us (18%)
  local copies, waits for them, and re-layouts  45.4 us (8%)
  other arithmetic  35.1 us (6%)
  starting transfers between devices  26.3 us (5%)
  matrix products  20.9 us (4%)
  between operations  14.8 us (3%)
    psum x1, waiting for transfers between devices, shards(): col_grad = lax.psum(col_part, 'row') / math.sqrt(total_rows)  196 us
    psum x1, waiting for transfers between devices, shards(): lax.psum(lax.psum((grad_one, bias_part, grad_two), 'row'), 'col')  96.6 us
    psum x1, blocking collectives, shards(): lax.psum((grad_one, bias_part, grad_two), 'row')  71.9 us
    psum x1, blocking collectives, shards(): row_grad = lax.psum(row_part, 'col') / math.sqrt(total_cols)  26.7 us
    ppermute x4, starting transfers between devices, extended(): lax.ppermute(lax.slice_in_dim(block, block.shape[dim] - width, None, axis...  19.8 us
    conv_general_dilated x11, local copies, waits for them, and re-layouts, conv_valid(): lax.conv_general_dilated(field[None], kernel, (1, 1), 'VALID', rhs_dilati...  18.6 us
    unnamed x40, local copies, waits for them, and re-layouts  17.6 us
    conv_general_dilated x3, matrix products, conv_valid(): lax.conv_general_dilated(field[None], kernel, (1, 1), 'VALID', rhs_dilati...  14.1 us
  transfers between devices with their start and end apart: 10, of which 3 were waited for; matrix products, arithmetic and copies ran while one was open for 9% of the time, Pallas kernels for 0%

profile of v1, /device:TPU:1, one launch (start us, length us, event | category | flops | bytes accessed | tf_op | source)
XLA Modules:
  0.0 538.8 jit_solution(9954317080476350708)
XLA Ops:
  7.2 4.2 collective-permute-start.4
  11.4 1.3 collective-permute-start.5
  12.7 0.8 fusion.84
  13.5 5.7 %collective-permute-start.6 = (bf16[16,64]{0,1:T(8,128)(2,1)S(1)}, bf16[16,64]{0,1:T(8,128)(2,1)S(1)}, u32[]{:S(2)}, u32[]{:S(2)}) collective-permute-start(bf16[16,64]{0,1:T(8,128)(2,1)S(1)} %get-tuple-element.27), channel_id=1, source_target_pairs={{0,1},{1,2},{2,3},{3,4},{4,5},{5,6},{6,7},{8,9},{9,10},{10,11},{11... | collective-permute-start | bytes 6152 | tf_op jit(solution)/shard_map/ppermute | solution.py:13
  19.3 1.9 collective-permute-start.7
  21.2 5.1 collective-permute-start
  26.5 3.6 copy.67
  30.4 1.3 collective-permute-start.1
  31.7 0.8 convert_bitcast_fusion
  32.7 0.7 convert_bitcast_fusion.1
  33.4 2.7 select_convert_fusion
  36.1 2.3 copy.77
  39.3 5.9 %broadcast_select_fusion = f32[32,8,36,64]{3,1,2,0:T(8,128)S(1)} fusion(pred[8,36]{0,1:T(8,128)(4,1)S(1)} %copy-done.15, bf16[3,3,64,64]{3,2,1,0:T(8,128)(2,1)S(1)} %copy-done.12, bf16[64,48,1,7,16]{0,3,4,1,2:T(8,128)(2,1)S(1)} %slice.100, bf16[64,48,1,8,36]{0,3,4,1,2:T(8,128)(2,1)S(1)} %copy.77), kind=kOutput, calls=%fused_computation.34 | convolution fusion | flops 687734784 | bytes 4890912 | tf_op jit(solution)/shard_map/conv_general_dilated | solution.py:22
  45.2 2.7 copy.84
  47.9 2.6 slice.105
  50.5 6.2 %copy.124 = f32[32,1,272,64]{2,3,0,1:T(8,128)} copy(f32[32,1,272,64]{3,0,2,1:T(8,128)} %slice.105) | data formatting | bytes 4456448
  56.7 3.2 select_convert_fusion.2
  63.5 2.3 select_convert_fusion.1
  66.5 3.8 add_divide_fusion
  70.3 3.6 copy.69
  73.8 3.6 copy.71
  77.4 1.2 pad_maximum_fusion.5
  78.7 4.8 collective-permute-start.2
  83.5 1.9 collective-permute-start.3
  85.4 0.7 pad_maximum_fusion.2
  86.2 5.2 collective-permute-done.3
  91.4 5.1 pad_maximum_fusion
  96.5 2.3 copy.73
  99.3 6.2 %multiply_multiply_fusion = (bf16[32,8,36,64]{3,1,2,0:T(8,128)(2,1)}, f32[32,8,36,64]{3,1,2,0:T(8,128)S(1)}) fusion(f32[32,8,36,64]{3,1,2,0:T(8,128)S(1)} %bitcast.164, f32[64]{0:T(128)S(1)} %copy-done.11, bf16[3,3,64,64]{3,2,1,0:T(8,128)(2,1)S(1)} %copy-done, bf16[64,48,1,7,16]{0,3,4,1,2:T(8,128)(2,1)S(1)} %slice.99, ...), kind=kOutput, calls=%fused_computation.18 | convolution fusion | flops 693633024 | bytes 8430112 | tf_op jit(solution)/shard_map/conv_general_dilated | solution.py:22
  105.5 2.7 copy.82
  108.2 2.5 slice.104
  110.8 6.2 %copy.123 = f32[32,1,272,64]{2,3,0,1:T(8,128)} copy(f32[32,1,272,64]{3,0,2,1:T(8,128)} %slice.104) | data formatting | bytes 4456448
  116.9 3.8 convert_reduce_fusion
  124.0 0.9 copy.78
  125.0 2.2 fusion.17
  127.2 1.4 copy.80
  129.0 2.0 fusion.33
  131.1 0.7 copy.81
  132.3 1.4 fusion.36
  133.7 0.7 pad_maximum_fusion.1
  134.5 71.9 %psum.60 = f32[64]{0:T(128)S(1)} all-reduce(f32[64]{0:T(128)S(1)} %get-tuple-element.21), channel_id=1, replica_groups=mesh['row'=32,'col'=8] {'row'}, use_global_device_ids=true, to_apply=%region_7.8 | all-reduce | flops 64 | bytes 512 | tf_op jit(solution)/shard_map/psum | solution.py:95
  206.4 26.7 %all-reduce.1 = (f32[16,64]{1,0:T(8,128)S(1)}, f32[64]{0:T(128)S(1)}) all-reduce(f32[16,64]{1,0:T(8,128)S(1)} %bitcast.166, f32[64]{0:T(128)S(1)} %psum.60), channel_id=1, replica_groups=mesh['row'=32,'col'=8] {'col'}, use_global_device_ids=true, to_apply=%region_1.2 | all-reduce | flops 1088 | bytes 8704 | tf_op jit(solution)/shard_map/psum | solution.py:93
  233.8 195.8 %all-reduce.6.cloned.1.call-done = (f32[256,64]{1,0:T(8,128)}, f32[3,3,64,64]{3,2,1,0:T(8,128)}, f32[3,3,64,64]{3,2,1,0:T(8,128)}) async-done(((f32[256,64]{1,0:T(8,128)}, f32[3,3,64,64]{3,2,1,0:T(8,128)}, f32[3,3,64,64]{3,2,1,0:T(8,128)}), (f32[256,64]{1,0:T(8,128)}, f32[3,3,64,64]{3,2,1,0:T(8,128)}, f32[3,3,64,64]{3,2,1,0:T(8,128)})) %all-reduce.6.cloned.1.call-update) | async-done | bytes 360464 | tf_op jit(solution)/shard_map/psum | solution.py:94
  430.1 0.9 broadcast_multiply_fusion.2
  431.0 0.7 copy.104
  431.8 96.6 %all-reduce.8.cloned.1.call-done = (f32[3,3,64,64]{3,2,1,0:T(8,128)}, f32[3,3,64,64]{3,2,1,0:T(8,128)}) async-done(((f32[3,3,64,64]{3,2,1,0:T(8,128)}, f32[3,3,64,64]{3,2,1,0:T(8,128)}), (f32[3,3,64,64]{3,2,1,0:T(8,128)}, f32[3,3,64,64]{3,2,1,0:T(8,128)})) %all-reduce.8.cloned.1.call-update) | async-done | bytes 294928 | tf_op jit(solution)/shard_map/psum | solution.py:95
  528.3 1.7 broadcast_multiply_fusion
  530.0 1.7 broadcast_multiply_fusion.1
  (85 shorter events, 11.6 us)
Async XLA Ops:
  7.2 92.1 %copy-start = (bf16[3,3,64,64]{3,2,1,0:T(8,128)(2,1)S(1)}, bf16[3,3,64,64]{3,2,1,0:T(8,128)(2,1)}, u32[]{:S(2)}) copy-start(bf16[3,3,64,64]{3,2,1,0:T(8,128)(2,1)} %param.11) | copy-start | bytes 221188
  7.2 422.4 %all-reduce.6.cloned.1.call-start = ((), (), s32[]{:S(2)}) async-start(), calls=%async_computation | async-start | bytes 1441792 | tf_op jit(solution)/shard_map/psum | solution.py:94
  7.2 25.5 %collective-permute-start.4 = (bf16[16,64]{1,0:T(8,128)(2,1)}, bf16[16,64]{1,0:T(8,128)(2,1)S(1)}, u32[]{:S(2)}, u32[]{:S(2)}) collective-permute-start(bf16[16,64]{1,0:T(8,128)(2,1)} %param.7), channel_id=1, source_target_pairs={{0,8},{8,16},{16,24},{24,32},{32,40},{40,48},{48,56},{56,64},{64,7... | collective-permute-start | bytes 6152 | tf_op jit(solution)/shard_map/ppermute | solution.py:13
  11.4 21.3 %collective-permute-start.5 = (bf16[16,64]{1,0:T(8,128)(2,1)}, bf16[16,64]{1,0:T(8,128)(2,1)S(1)}, u32[]{:S(2)}, u32[]{:S(2)}) collective-permute-start(bf16[16,64]{1,0:T(8,128)(2,1)} %param.7), channel_id=1, source_target_pairs={{8,0},{16,8},{24,16},{32,24},{40,32},{48,40},{56,48},{64,56},{72,6... | collective-permute-start | bytes 6152 | tf_op jit(solution)/shard_map/ppermute | solution.py:16
  13.5 16.9 %collective-permute-start.6 = (bf16[16,64]{0,1:T(8,128)(2,1)S(1)}, bf16[16,64]{0,1:T(8,128)(2,1)S(1)}, u32[]{:S(2)}, u32[]{:S(2)}) collective-permute-start(bf16[16,64]{0,1:T(8,128)(2,1)S(1)} %get-tuple-element.27), channel_id=1, source_target_pairs={{0,1},{1,2},{2,3},{3,4},{4,5},{5,6},{6,7},{8,9},{9,10},{10,11},{11... | collective-permute-start | bytes 6152 | tf_op jit(solution)/shard_map/ppermute | solution.py:13
  19.3 12.5 %collective-permute-start.7 = (bf16[16,64]{0,1:T(8,128)(2,1)S(1)}, bf16[16,64]{0,1:T(8,128)(2,1)S(1)}, u32[]{:S(2)}, u32[]{:S(2)}) collective-permute-start(bf16[16,64]{0,1:T(8,128)(2,1)S(1)} %get-tuple-element.28), channel_id=1, source_target_pairs={{1,0},{2,1},{3,2},{4,3},{5,4},{6,5},{7,6},{9,8},{10,9},{11,10},{12... | collective-permute-start | bytes 6152 | tf_op jit(solution)/shard_map/ppermute | solution.py:16
  21.2 49.1 %collective-permute-start = (bf16[64,16,256]{2,1,0:T(8,128)(2,1)}, bf16[64,16,256]{2,1,0:T(8,128)(2,1)}, u32[]{:S(2)}, u32[]{:S(2)}) collective-permute-start(bf16[64,16,256]{2,1,0:T(8,128)(2,1)} %param.6), channel_id=1, source_target_pairs={{0,8},{8,16},{16,24},{24,32},{32,40},{40,48},{48,56},{56,64},{64,7... | collective-permute-start | bytes 1572872 | tf_op jit(solution)/shard_map/ppermute | solution.py:13
  30.4 43.4 %collective-permute-start.1 = (bf16[64,16,256]{2,1,0:T(8,128)(2,1)}, bf16[64,16,256]{2,1,0:T(8,128)(2,1)}, u32[]{:S(2)}, u32[]{:S(2)}) collective-permute-start(bf16[64,16,256]{2,1,0:T(8,128)(2,1)} %param.6), channel_id=1, source_target_pairs={{8,0},{16,8},{24,16},{32,24},{40,32},{48,40},{56,48},{64,56},{72,6... | collective-permute-start | bytes 1572872 | tf_op jit(solution)/shard_map/ppermute | solution.py:16
  38.4 0.9 copy-start.12
  38.4 0.9 copy-start.15
  45.2 2.8 copy-start.6
  50.5 6.2 %copy-start.11 = (f32[64]{0:T(128)S(1)}, f32[64]{0:T(128)}, u32[]{:S(2)}) copy-start(f32[64]{0:T(128)} %param.10) | copy-start | bytes 772
  56.7 3.2 copy-start.9
  77.4 8.0 %copy-start.10 = (f32[1,3,64,64]{3,2,1,0:T(8,128)S(1)}, f32[1,3,64,64]{3,2,1,0:T(8,128)}, u32[]{:S(2)}) copy-start(f32[1,3,64,64]{3,2,1,0:T(8,128)} %get-tuple-element.34) | copy-start | bytes 147460
  77.4 14.0 %copy-start.2 = (bf16[64,16,256]{0,1,2:T(8,128)(2,1)S(1)}, bf16[64,16,256]{0,1,2:T(8,128)(2,1)}, u32[]{:S(2)}) copy-start(bf16[64,16,256]{0,1,2:T(8,128)(2,1)} %copy.67) | copy-start | bytes 1572868
  77.4 14.0 %copy-start.4 = (bf16[64,16,256]{0,1,2:T(8,128)(2,1)S(1)}, bf16[64,16,256]{0,1,2:T(8,128)(2,1)}, u32[]{:S(2)}) copy-start(bf16[64,16,256]{0,1,2:T(8,128)(2,1)} %copy.69) | copy-start | bytes 1572868
  77.4 14.0 %copy-start.5 = (bf16[64,16,256]{0,1,2:T(8,128)(2,1)S(1)}, bf16[64,16,256]{0,1,2:T(8,128)(2,1)}, u32[]{:S(2)}) copy-start(bf16[64,16,256]{0,1,2:T(8,128)(2,1)} %copy.71) | copy-start | bytes 1572868
  78.7 7.5 %collective-permute-start.2 = (bf16[64,48,16]{0,1,2:T(8,128)(2,1)S(1)}, bf16[64,48,16]{0,1,2:T(8,128)(2,1)S(1)}, u32[]{:S(2)}, u32[]{:S(2)}) collective-permute-start(bf16[64,48,16]{0,1,2:T(8,128)(2,1)S(1)} %get-tuple-element.25), channel_id=1, source_target_pairs={{0,1},{1,2},{2,3},{3,4},{4,5},{5,6},{6,7},{8,9},{9,10},{10,11},{11... | collective-permute-start | bytes 294920 | tf_op jit(solution)/shard_map/ppermute | solution.py:13
  83.5 7.9 %collective-permute-start.3 = (bf16[64,48,16]{0,1,2:T(8,128)(2,1)S(1)}, bf16[64,48,16]{0,1,2:T(8,128)(2,1)S(1)}, u32[]{:S(2)}, u32[]{:S(2)}) collective-permute-start(bf16[64,48,16]{0,1,2:T(8,128)(2,1)S(1)} %get-tuple-element.26), channel_id=1, source_target_pairs={{1,0},{2,1},{3,2},{4,3},{5,4},{6,5},{7,6},{9,8},{10,9},{11,10},{12... | collective-permute-start | bytes 294920 | tf_op jit(solution)/shard_map/ppermute | solution.py:16
  91.4 7.9 %slice-start = ((s8[4718592]{0:T(1024)(128)(4,1)}), s8[4194304]{0:T(1024)(128)(4,1)S(1)}, s32[]{:S(2)}) async-start(s8[4718592]{0:T(1024)(128)(4,1)} %bitcast.163), calls=%async_computation.2 | async-start | bytes 8388608
  96.5 2.8 slice-start.1
  116.9 3.8 copy-start.7
  121.8 2.2 copy-start.8
  127.2 1.8 copy-start.13
  127.2 1.8 copy-start.14
  131.1 1.2 copy-start.3
  131.8 399.9 %copy-start.1 = (bf16[3,3,64,64]{3,2,1,0:T(8,128)(2,1)S(1)}, bf16[3,3,64,64]{3,2,1,0:T(8,128)(2,1)}, u32[]{:S(2)}) copy-start(bf16[3,3,64,64]{3,2,1,0:T(8,128)(2,1)} %param.11) | copy-start | bytes 221188
  134.5 393.8 %all-reduce.8.cloned.1.call-start = ((), (), s32[]{:S(2)}) async-start(), calls=%async_computation.1 | async-start | bytes 1179648 | tf_op jit(solution)/shard_map/psum | solution.py:95
Sparse Core Ops, SparseCore 0:
  134.6 294.9 all-reduce.5
  432.5 95.8 all-reduce.7
